TPU v7x, 256 devices: a whole 4x4x8 slice. The times are simulated.
256 devices in a mesh: tower: 8 (over x, core), peer: 32 (over z, y).
Axes of the slice: x: 4, y: 4, z: 8, core: 2. Of those that a mesh axis runs over, the one named last changes fastest.
Arguments:
- embeddings: bfloat16 [16384, 2048], P('tower', 'peer'), may hold values from -6 to 6
- session_lists: int32 [8, 2048], P('tower'), may hold values from 0 to 2047, each once within a row
- owners: int32 [16384, 1], P(('tower', 'peer')), may hold values from 0 to 7; in each aligned block of 64 rows (0 to 63, 64 to 127, ...) at most 16 rows name the same one
- counts: int32 [16384], P(('tower', 'peer')), may hold values from 1 to 3, as said below
- item_feats: bfloat16 [98304, 256], P(('tower', 'peer')), may hold values from -6 to 6
- cotangent: bfloat16 [98304, 1024], P(('tower', 'peer')), may hold values from -6 to 6
- cross_down: bfloat16 [2048, 256], replicated, may hold values from -0.125 to 0.125
- cross_up: bfloat16 [256, 2048], replicated, may hold values from -0.375 to 0.375
- compress: bfloat16 [2048, 256], replicated, may hold values from -0.125 to 0.125
- over_first: bfloat16 [512, 4096], replicated, may hold values from -0.25 to 0.25
- over_second: bfloat16 [4096, 1024], P('peer'), may hold values from -0.09375 to 0.09375
- over_third: bfloat16 [1024, 1024], replicated, may hold values from -0.1875 to 0.1875
Outputs:
- over_out: bfloat16 [98304, 1024], P(('tower', 'peer'))
- emb_grad: bfloat16 [16384, 2048], P('tower', 'peer')
Inputs may be any that keep to these rules, and one draw needn't show every extreme that they name: `session_lists`: each row is a permutation of the tower's 64 * 32 table rows. `owners`: within the 64 sessions of one device, no tower owns more than 16 of them. `counts`: the first session of every device has 3 samples and the second has one.
All inputs are finite; a program needn't handle non-finite values.
Results may differ from a plain program's by a relative error of at most 0.02.
Values may be sent and summed in bfloat16 or wider, within the bound.
A program may use at most 128 MiB of HBM per device.

v0:
```python
import jax
import jax.numpy as jnp
from jax import lax
from jax.sharding import PartitionSpec as P

MOSTC = 3


def silu_slope(pre):
    sigma = jax.nn.sigmoid(pre)
    return sigma * (1.0 + pre * (1.0 - sigma))


def times_t(left, right):
    return lax.dot_general(
        left, right, (((1,), (1,)), ((), ())), preferred_element_type=jnp.float32
    )


def body(
    embeddings,
    session_lists,
    owners,
    counts,
    item_feats,
    cotangent,
    cross_down,
    cross_up,
    compress,
    over_first,
    over_second,
    over_third,
):
    towers = lax.axis_size("tower")
    comp_width = compress.shape[1]
    grid_rows = item_feats.shape[0]
    slots = grid_rows // (towers * MOSTC)
    order = session_lists[0]
    picked = jnp.take(embeddings, order, axis=0)
    session_rows = lax.all_to_all(picked, "peer", split_axis=0, concat_axis=1, tiled=True)
    low = jnp.dot(session_rows, cross_down, preferred_element_type=jnp.float32).astype(jnp.bfloat16)
    lift = jnp.dot(low, cross_up, preferred_element_type=jnp.float32)
    rows_wide = session_rows.astype(jnp.float32)
    crossed = (rows_wide * lift + rows_wide).astype(jnp.bfloat16)
    compressed = jnp.dot(crossed, compress, preferred_element_type=jnp.float32).astype(jnp.bfloat16)
    owner_list = owners[:, 0]
    choose = (owner_list[:, None] == jnp.arange(towers, dtype=jnp.int32)[None, :]).astype(jnp.int32)
    earlier = jnp.cumsum(choose, axis=0) - choose
    position = jnp.sum(choose * earlier, axis=1)
    target = owner_list * slots + position
    dispatch = (target[:, None] == jnp.arange(towers * slots, dtype=jnp.int32)[None, :]).astype(
        jnp.int32
    )
    dispatch_half = dispatch.astype(jnp.bfloat16)
    send_rows = lax.dot_general(
        dispatch_half, compressed, (((0,), (0,)), ((), ())), preferred_element_type=jnp.float32
    ).astype(jnp.bfloat16)
    send_counts = jnp.sum(dispatch * counts[:, None], axis=0)
    repeated = jnp.broadcast_to(send_rows[:, None, :], (towers * slots, MOSTC, comp_width))
    repeated = repeated.reshape(towers, slots * MOSTC, comp_width)
    got_rows, got_counts = (
        lax.all_to_all(repeated, "tower", split_axis=0, concat_axis=0, tiled=True),
        lax.all_to_all(
            send_counts.reshape(towers, slots), "tower", split_axis=0, concat_axis=0, tiled=True
        ),
    )
    expanded = got_rows.reshape(grid_rows, comp_width)
    live = (
        jnp.arange(MOSTC, dtype=jnp.int32)[None, :] < got_counts.reshape(towers * slots)[:, None]
    ).astype(jnp.float32)
    live = live.reshape(grid_rows)
    inputs = jnp.concatenate([expanded, item_feats], axis=1)
    pre_first = jnp.dot(inputs, over_first, preferred_element_type=jnp.float32)
    hidden_first = jax.nn.silu(pre_first).astype(jnp.bfloat16)
    pre_second = jnp.dot(
        hidden_first,
        lax.all_gather(over_second, "peer", axis=0, tiled=True),
        preferred_element_type=jnp.float32,
    )
    hidden_second = jax.nn.silu(pre_second).astype(jnp.bfloat16)
    over_out = (
        jnp.dot(hidden_second, over_third, preferred_element_type=jnp.float32) * live[:, None]
    ).astype(jnp.bfloat16)
    masked = cotangent * live[:, None].astype(jnp.bfloat16)
    grad_second = (times_t(masked, over_third) * silu_slope(pre_second)).astype(jnp.bfloat16)
    back_first = times_t(grad_second, lax.all_gather(over_second, "peer", axis=0, tiled=True))
    grad_first = (back_first * silu_slope(pre_first)).astype(jnp.bfloat16)
    sample_grad = times_t(grad_first, over_first[:comp_width]).astype(jnp.bfloat16)
    returned = lax.all_to_all(
        sample_grad.reshape(towers, slots * MOSTC, comp_width),
        "tower",
        split_axis=0,
        concat_axis=0,
        tiled=True,
    )
    slot_grad = jnp.sum(
        returned.astype(jnp.float32).reshape(towers * slots, MOSTC, comp_width), axis=1
    ).astype(jnp.bfloat16)
    session_grad = jnp.dot(dispatch_half, slot_grad, preferred_element_type=jnp.float32).astype(
        jnp.bfloat16
    )
    grad_crossed = times_t(session_grad, compress).astype(jnp.bfloat16)
    grad_lift = (grad_crossed.astype(jnp.float32) * rows_wide).astype(jnp.bfloat16)
    grad_low = times_t(grad_lift, cross_up).astype(jnp.bfloat16)
    grad_rows = (
        grad_crossed.astype(jnp.float32) * (lift + 1.0) + times_t(grad_low, cross_down)
    ).astype(jnp.bfloat16)
    columns_back = lax.all_to_all(grad_rows, "peer", split_axis=1, concat_axis=0, tiled=True)
    emb_grad = jnp.zeros_like(embeddings).at[order].set(columns_back)
    return (over_out, emb_grad)


def solution(mesh):
    return jax.shard_map(
        body,
        mesh=mesh,
        in_specs=(
            P("tower", "peer"),
            P("tower", None),
            P(("tower", "peer"), None),
            P(("tower", "peer")),
            P(("tower", "peer"), None),
            P(("tower", "peer"), None),
            P(),
            P(),
            P(),
            P(),
            P("peer", None),
            P(),
        ),
        out_specs=(P(("tower", "peer"), None), P("tower", "peer")),
        check_vma=False,
    )
```

profile of v0, /device:TPU:32, one launch (start us, length us, event | category | flops | bytes accessed | tf_op | source)
XLA Modules:
  0.0 187.4 jit_solution(9144501375350728294)
XLA Ops:
  7.2 0.0 copy-start
  7.2 0.0 all-gather.2.cloned.1.call-start
  7.2 0.7 all-gather.2.cloned.1.call-update
  7.9 0.7 fusion.25
  8.6 0.1 reduce_window_sum.11
  8.7 0.8 select_reduce_fusion.1
  9.6 0.7 fusion.29
  10.2 0.7 select_reduce_fusion
  11.0 0.7 all_to_all.42
  11.7 4.3 %all-to-all-start.2 = ((s32[8,1,16]{2,1,0:T(1,128)}), s32[8,1,16]{2,1,0:T(1,128)S(1)}, u32[]{:S(2)}, u32[]{:S(2)}) async-start(s32[8,1,16]{2,1,0:T(1,128)} %bitcast.8), calls=%async_computation.2 | async-start | bytes 8192 | tf_op jit(solution)/shard_map/all_to_all | solution.py:63
  16.0 1.2 copy.28
  17.2 0.5 broadcast.66
  17.7 1.3 reduce.7
  19.0 0.1 squeeze.6
  19.1 0.7 compare_select_fusion
  19.8 6.2 %gather_fusion = bf16[2048,64]{1,0:T(8,128)(2,1)S(1)} fusion(bf16[2048,64]{1,0:T(8,128)(2,1)S(1)} %copy.28, s32[2048]{0:T(1024)S(1)} %broadcast_clamp_fusion), kind=kCustom, calls=%fused_computation | custom fusion | bytes 532480 | tf_op jit(solution)/shard_map/jit(_take)/gather | solution.py:39
  26.0 0.3 broadcast_select_fusion
  26.3 1.1 reshape.142
  27.4 0.0 all-to-all-done.2
  27.4 11.4 %all-to-all-start = ((bf16[32,2,2048]{2,1,0:T(2,128)(2,1)}), bf16[32,2,2048]{2,1,0:T(2,128)(2,1)S(1)}, u32[]{:S(2)}, u32[]{:S(2)}) async-start(bf16[32,2,2048]{2,1,0:T(2,128)(2,1)} %reshape.142), calls=%async_computation | async-start | bytes 524288 | tf_op jit(solution)/shard_map/all_to_all | solution.py:40
  38.8 0.6 reduce.8
  39.4 0.1 lt.53
  39.5 14.4 %all-to-all-done = bf16[32,2,2048]{2,1,0:T(2,128)(2,1)S(1)} async-done(((bf16[32,2,2048]{2,1,0:T(2,128)(2,1)}), bf16[32,2,2048]{2,1,0:T(2,128)(2,1)S(1)}, u32[]{:S(2)}, u32[]{:S(2)}) %all-to-all-start) | async-done | bytes 262176 | tf_op jit(solution)/shard_map/all_to_all | solution.py:40
  53.9 0.4 reshape.143
  54.3 0.3 copy.29
  54.6 0.5 all_to_all.40
  55.1 0.0 copy-start.1
  55.1 2.4 %fusion.8 = f32[64,2048]{1,0:T(8,128)S(1)} fusion(bf16[256,2048]{1,0:T(8,128)(2,1)} %param.19, bf16[64,2048]{1,0:T(8,128)(2,1)S(1)} %all_to_all.40, bf16[2048,256]{1,0:T(8,128)(2,1)} %param.18), kind=kOutput, calls=%fused_computation.22 | convolution fusion | flops 134234112 | bytes 2883584 | tf_op jit(solution)/shard_map/dot_general | solution.py:42
  57.5 1.7 convolution_convert_fusion.1
  59.2 0.1 broadcast_in_dim.16
  59.2 0.8 reshape.102
  60.1 4.5 %all-to-all-start.1 = ((bf16[8,48,256]{2,1,0:T(8,128)(2,1)}), bf16[8,48,256]{2,1,0:T(8,128)(2,1)S(1)}, u32[]{:S(2)}, u32[]{:S(2)}) async-start(bf16[8,48,256]{2,1,0:T(8,128)(2,1)} %reshape.102), calls=%async_computation.1 | async-start | bytes 393216 | tf_op jit(solution)/shard_map/all_to_all | solution.py:62
  64.6 0.1 fusion.24
  64.7 0.2 reshape.107
  64.9 6.5 %all-to-all-done.1 = bf16[8,48,256]{2,1,0:T(8,128)(2,1)S(1)} async-done(((bf16[8,48,256]{2,1,0:T(8,128)(2,1)}), bf16[8,48,256]{2,1,0:T(8,128)(2,1)S(1)}, u32[]{:S(2)}, u32[]{:S(2)}) %all-to-all-start.1) | async-done | bytes 196640 | tf_op jit(solution)/shard_map/all_to_all | solution.py:62
  71.4 0.0 copy-done.1
  71.4 6.7 %fusion.13 = f32[384,4096]{1,0:T(8,128)} fusion(bf16[512,4096]{1,0:T(8,128)(2,1)} %param.21, bf16[384,256]{1,0:T(8,128)(2,1)S(1)} %copy-done.1, bf16[384,256]{1,0:T(8,128)(2,1)S(1)} %bitcast.39), kind=kOutput, calls=%fused_computation.30 | convolution fusion | flops 1611399168 | bytes 10878976 | tf_op jit(solution)/shard_map/dot_general | solution.py:73
  78.1 34.4 %all-gather.2.cloned.1.call-done = bf16[4096,1024]{1,0:T(8,128)(2,1)} async-done(((bf16[128,1024]{1,0:T(8,128)(2,1)}), bf16[4096,1024]{1,0:T(8,128)(2,1)}) %all-gather.2.cloned.1.call-update) | async-done | bytes 8388624 | tf_op jit(solution)/shard_map/all_gather | solution.py:77
  112.5 0.0 copy-start.2
  112.5 8.1 %fusion = f32[384,1024]{1,0:T(8,128)S(1)} fusion(bf16[4096,1024]{1,0:T(8,128)(2,1)} %all-gather.2.cloned.1.call-done, f32[384,4096]{1,0:T(8,128)} %fusion.13), kind=kOutput, calls=%fused_computation.5 | convolution fusion | flops 3229089792 | bytes 16252928 | tf_op jit(solution)/shard_map/dot_general | solution.py:75
  120.7 0.0 copy-start.3
  120.7 1.2 copy-done.3
  121.8 0.0 copy-done
  121.8 0.0 copy-done.2
  121.8 2.1 %multiply_convert_fusion.3 = bf16[384,1024]{1,0:T(8,128)(2,1)} fusion(f32[384,1024]{1,0:T(8,128)S(1)} %fusion, bf16[1024,1024]{1,0:T(8,128)(2,1)S(1)} %copy-done, bf16[384,1024]{1,0:T(8,128)(2,1)S(1)} %copy-done.2, bf16[384]{0:T(512)(128)(2,1)S(1)} %convert_element_type.100), kind=kOutput, calls=%fused_computation.12 | convolution fusion | flops 809238528 | bytes 5243648 | tf_op jit(solution)/shard_map/dot_general | solution.py:15
  124.0 10.5 %fusion.5 = bf16[384,256]{1,0:T(8,128)(2,1)S(1)} fusion(bf16[512,4096]{1,0:T(8,128)(2,1)} %param.21, f32[384,4096]{1,0:T(8,128)} %fusion.13, bf16[384,1024]{1,0:T(8,128)(2,1)} %multiply_convert_fusion.3, bf16[4096,1024]{1,0:T(8,128)(2,1)} %all-gather.2.cloned.1.call-done), kind=kOutput, calls=%fused_computation.16 | convolution fusion | flops 4040785920 | bytes 17760256 | tf_op jit(solution)/shard_map/dot_general | solution.py:15
  134.5 10.9 %all_to_all.54 = bf16[8,48,256]{2,1,0:T(8,128)(2,1)S(1)} all-to-all(bf16[8,48,256]{2,1,0:T(8,128)(2,1)S(1)} %bitcast.41), channel_id=1, replica_groups=mesh['tower'=8,'peer'=32] {'tower'}, dimensions={0} | all-to-all | bytes 393216 | tf_op jit(solution)/shard_map/all_to_all | solution.py:89
  145.4 0.1 reshape.105
  145.5 0.3 reduce
  145.9 1.8 fusion.2
  147.6 3.5 %fusion.1 = bf16[64,2048]{1,0:T(8,128)(2,1)} fusion(bf16[2048,256]{1,0:T(8,128)(2,1)} %param.18, bf16[256,2048]{1,0:T(8,128)(2,1)} %param.19, f32[64,2048]{1,0:T(8,128)S(1)} %fusion.2, f32[64,2048]{1,0:T(8,128)S(1)} %fusion.8, bf16[64,2048]{1,0:T(8,128)(2,1)S(1)} %all_to_all.40), kind=kOutput, calls=%fused_computation.7 | convolution fusion | flops 135151616 | bytes 3670016 | tf_op jit(solution)/shard_map/dot_general | solution.py:15
  151.2 1.5 all_to_all.45
  152.6 0.2 copy.34
  152.8 1.1 reshape.144
  153.9 7.6 %all-to-all-start.4 = ((bf16[32,2,2048]{2,1,0:T(2,128)(2,1)}), bf16[32,2,2048]{2,1,0:T(2,128)(2,1)S(1)}, u32[]{:S(2)}, u32[]{:S(2)}) async-start(bf16[32,2,2048]{2,1,0:T(2,128)(2,1)} %reshape.144), calls=%async_computation.4 | async-start | bytes 524288 | tf_op jit(solution)/shard_map/all_to_all | solution.py:108
  161.6 3.3 %multiply_convert_fusion.4 = bf16[384,1024]{1,0:T(8,128)(2,1)} fusion(bf16[1024,1024]{1,0:T(8,128)(2,1)S(1)} %copy-done, f32[384,1024]{1,0:T(8,128)} %copy-done.3, f32[384]{0:T(512)S(1)} %reshape.107), kind=kOutput, calls=%fused_computation.13 | convolution fusion | flops 808058880 | bytes 4457984 | tf_op jit(solution)/shard_map/dot_general | solution.py:82
  164.9 8.5 %all-to-all-done.4 = bf16[32,2,2048]{2,1,0:T(2,128)(2,1)S(1)} async-done(((bf16[32,2,2048]{2,1,0:T(2,128)(2,1)}), bf16[32,2,2048]{2,1,0:T(2,128)(2,1)S(1)}, u32[]{:S(2)}, u32[]{:S(2)}) %all-to-all-start.4) | async-done | bytes 262176 | tf_op jit(solution)/shard_map/all_to_all | solution.py:108
  173.4 0.4 reshape.145
  173.8 5.9 %scatter_custom_fusion = bf16[2048,64]{1,0:T(8,128)(2,1)S(1)} fusion(s32[2048]{0:T(1024)S(1)} %bitcast.43, bf16[2048,64]{1,0:T(8,128)(2,1)S(1)} %bitcast.40, bf16[]{:T(256)} %constant.36.clone.1), kind=kCustom, calls=%fused_computation.35 | custom fusion | bytes 262146 | tf_op jit(solution)/shard_map/scatter | solution.py:109
  179.6 0.9 copy.32
  (3 shorter events, 0.0 us)
Async XLA Ops:
  7.2 114.7 %copy-start = (bf16[1024,1024]{1,0:T(8,128)(2,1)S(1)}, bf16[1024,1024]{1,0:T(8,128)(2,1)}, u32[]{:S(2)}) copy-start(bf16[1024,1024]{1,0:T(8,128)(2,1)} %param.23) | copy-start | bytes 6291460
  7.2 105.4 %all-gather.2.cloned.1.call-start = ((), (), s32[]{:S(2)}) async-start(), calls=%async_computation.5 | async-start | bytes 8650752 | tf_op jit(solution)/shard_map/all_gather | solution.py:77
  11.7 15.8 %all-to-all-start.2 = ((s32[8,1,16]{2,1,0:T(1,128)}), s32[8,1,16]{2,1,0:T(1,128)S(1)}, u32[]{:S(2)}, u32[]{:S(2)}) async-start(s32[8,1,16]{2,1,0:T(1,128)} %bitcast.8), calls=%async_computation.2 | async-start | bytes 8192 | tf_op jit(solution)/shard_map/all_to_all | solution.py:63
  27.4 26.5 %all-to-all-start = ((bf16[32,2,2048]{2,1,0:T(2,128)(2,1)}), bf16[32,2,2048]{2,1,0:T(2,128)(2,1)S(1)}, u32[]{:S(2)}, u32[]{:S(2)}) async-start(bf16[32,2,2048]{2,1,0:T(2,128)(2,1)} %reshape.142), calls=%async_computation | async-start | bytes 524288 | tf_op jit(solution)/shard_map/all_to_all | solution.py:40
  55.1 16.3 %copy-start.1 = (bf16[384,256]{1,0:T(8,128)(2,1)S(1)}, bf16[384,256]{1,0:T(8,128)(2,1)}, u32[]{:S(2)}) copy-start(bf16[384,256]{1,0:T(8,128)(2,1)} %param.16) | copy-start | bytes 589828
  60.1 11.3 %all-to-all-start.1 = ((bf16[8,48,256]{2,1,0:T(8,128)(2,1)}), bf16[8,48,256]{2,1,0:T(8,128)(2,1)S(1)}, u32[]{:S(2)}, u32[]{:S(2)}) async-start(bf16[8,48,256]{2,1,0:T(8,128)(2,1)} %reshape.102), calls=%async_computation.1 | async-start | bytes 393216 | tf_op jit(solution)/shard_map/all_to_all | solution.py:62
  112.5 9.3 %copy-start.2 = (bf16[384,1024]{1,0:T(8,128)(2,1)S(1)}, bf16[384,1024]{1,0:T(8,128)(2,1)}, u32[]{:S(2)}) copy-start(bf16[384,1024]{1,0:T(8,128)(2,1)} %param.17) | copy-start | bytes 2359300
  120.7 1.2 copy-start.3
  153.9 19.5 %all-to-all-start.4 = ((bf16[32,2,2048]{2,1,0:T(2,128)(2,1)}), bf16[32,2,2048]{2,1,0:T(2,128)(2,1)S(1)}, u32[]{:S(2)}, u32[]{:S(2)}) async-start(bf16[32,2,2048]{2,1,0:T(2,128)(2,1)} %reshape.144), calls=%async_computation.4 | async-start | bytes 524288 | tf_op jit(solution)/shard_map/all_to_all | solution.py:108
Sparse Core Ops, SparseCore 0:
  10.6 101.8 all-gather.1
where the time goes:
time: 188 us; the launch traced here: 187 us
  waiting for transfers between devices  64.6 us (34%)
  matrix products  40.1 us (21%)
  starting transfers between devices  27.8 us (15%)
  local copies, waits for them, and re-layouts  23.3 us (12%)
  between operations  14.2 us (8%)
  blocking collectives  10.9 us (6%)
  other arithmetic  6.42 us (3%)
    all_gather x1, waiting for transfers between devices, body(): lax.all_gather(over_second, 'peer', axis=0, tiled=True)  34.4 us
    dot_general x4, matrix products, times_t(): lax.dot_general(left, right, (((1,), (1,)), ((), ())), preferred_element_...  18 us
    all_to_all x1, waiting for transfers between devices, body(): lax.all_to_all(picked, 'peer', split_axis=0, concat_axis=1, tiled=True)  14.4 us
    all_to_all x1, starting transfers between devices, body(): lax.all_to_all(picked, 'peer', split_axis=0, concat_axis=1, tiled=True)  11.4 us
    all_to_all x1, blocking collectives, body(): lax.all_to_all(sample_grad.reshape(towers, slots * MOSTC, comp_width), 't...  10.9 us
    all_to_all x1, waiting for transfers between devices, body(): lax.all_to_all(grad_rows, 'peer', split_axis=1, concat_axis=0, tiled=True)  8.52 us
    dot_general x1, matrix products, body(): jnp.dot(hidden_first, lax.all_gather(over_second, 'peer', axis=0, tiled=T...  8.1 us
    all_to_all x1, starting transfers between devices, body(): lax.all_to_all(grad_rows, 'peer', split_axis=1, concat_axis=0, tiled=True)  7.63 us
  transfers between devices with their start and end apart: 5, of which 4 were waited for; matrix products, arithmetic and copies ran while one was open for 17% of the time, Pallas kernels for 0%

commit v1 on v0

--- a/solution.py
+++ b/solution.py
@@ -4,6 +4,13 @@
 from jax.sharding import PartitionSpec as P
 
 MOSTC = 3
+
+
+def all_by_exchange(x, name, dim):
+    size = lax.axis_size(name)
+    shards = jnp.stack([x for _ in range(size)])
+    shards = lax.all_to_all(shards, name, split_axis=0, concat_axis=0)
+    return jnp.concatenate(shards, axis=dim)
 
 
 def silu_slope(pre):
@@ -73,9 +80,7 @@
     pre_first = jnp.dot(inputs, over_first, preferred_element_type=jnp.float32)
     hidden_first = jax.nn.silu(pre_first).astype(jnp.bfloat16)
     pre_second = jnp.dot(
-        hidden_first,
-        lax.all_gather(over_second, "peer", axis=0, tiled=True),
-        preferred_element_type=jnp.float32,
+        hidden_first, all_by_exchange(over_second, "peer", 0), preferred_element_type=jnp.float32
     )
     hidden_second = jax.nn.silu(pre_second).astype(jnp.bfloat16)
     over_out = (

time: 188 us -> 384 us (2.04)
  waiting for transfers between devices: 64.6 us -> 246 us
  blocking collectives: 10.9 us -> 20.9 us
  local copies, waits for them, and re-layouts: 23.3 us -> 27.8 us
    all_to_all x1, waiting for transfers between devices: 6.53 us -> 226 us  [all_by_exchange(): shards = lax.all_to_all(shards, name, split_axis=0, concat_axis=0)]
    all_gather x1, waiting for transfers between devices: 34.4 us -> 0.01 us  [body(): lax.all_gather(over_second, 'peer', axis=0, tiled=True)]
    all_to_all x0 -> x1, blocking collectives: none -> 11.6 us  [body(): lax.all_to_all(repeated, 'tower', split_axis=0, concat_axis=0, tiled=True)]
    another operation x0 -> x1, local copies, waits for them, and re-layouts: none -> 4.29 us  [all_by_exchange(): shards = jnp.stack([x for _ in range(size)])]
  transfers between devices with their start and end apart: 5 -> 5, of which waited for: 4 -> 3; matrix products, arithmetic and copies ran while one was open for 17% -> 7% of each run, Pallas kernels for 0% -> 0%
where the time goes in v1:
time: 384 us; the launch traced here: 383 us
  waiting for transfers between devices  246 us (64%)
  matrix products  40.1 us (10%)
  starting transfers between devices  30.5 us (8%)
  local copies, waits for them, and re-layouts  27.8 us (7%)
  blocking collectives  20.9 us (5%)
  between operations  14.3 us (4%)
  other arithmetic  3.92 us (1%)
    all_to_all x1, waiting for transfers between devices, all_by_exchange(): shards = lax.all_to_all(shards, name, split_axis=0, concat_axis=0)  226 us
    dot_general x4, matrix products, times_t(): lax.dot_general(left, right, (((1,), (1,)), ((), ())), preferred_element_...  18 us
    all_to_all x1, blocking collectives, body(): lax.all_to_all(repeated, 'tower', split_axis=0, concat_axis=0, tiled=True)  11.6 us
    all_to_all x1, starting transfers between devices, body(): lax.all_to_all(picked, 'peer', split_axis=0, concat_axis=1, tiled=True)  11.4 us
    all_to_all x1, waiting for transfers between devices, body(): lax.all_to_all(picked, 'peer', split_axis=0, concat_axis=1, tiled=True)  11 us
    all_to_all x1, blocking collectives, body(): lax.all_to_all(sample_grad.reshape(towers, slots * MOSTC, comp_width), 't...  9.23 us
    all_to_all x1, starting transfers between devices, body(): lax.all_to_all(grad_rows, 'peer', split_axis=1, concat_axis=0, tiled=True)  9.12 us
    all_to_all x1, waiting for transfers between devices, body(): lax.all_to_all(grad_rows, 'peer', split_axis=1, concat_axis=0, tiled=True)  8.53 us
  transfers between devices with their start and end apart: 5, of which 3 were waited for; matrix products, arithmetic and copies ran while one was open for 7% of the time, Pallas kernels for 0%

profile of v1, /device:TPU:32, one launch (start us, length us, event | category | flops | bytes accessed | tf_op | source)
XLA Modules:
  0.0 383.2 jit_solution(16028255149472484777)
XLA Ops:
  7.2 0.0 copy-start
  7.2 0.0 copy-start.3
  7.2 0.0 copy-start.5
  7.2 1.4 copy.28
  8.6 0.7 compare_select_fusion
  9.3 0.5 broadcast.68
  9.8 1.3 reduce.7
  11.2 0.1 squeeze.6
  11.3 6.2 %gather_fusion = bf16[2048,64]{1,0:T(8,128)(2,1)S(1)} fusion(bf16[2048,64]{1,0:T(8,128)(2,1)S(1)} %copy.28, s32[2048]{0:T(1024)S(1)} %broadcast_clamp_fusion), kind=kCustom, calls=%fused_computation | custom fusion | bytes 532480 | tf_op jit(solution)/shard_map/jit(_take)/gather | solution.py:46
  17.4 0.3 broadcast_select_fusion
  17.8 1.1 reshape.148
  18.9 11.4 %all-to-all-start = ((bf16[32,2,2048]{2,1,0:T(2,128)(2,1)}), bf16[32,2,2048]{2,1,0:T(2,128)(2,1)S(1)}, u32[]{:S(2)}, u32[]{:S(2)}) async-start(bf16[32,2,2048]{2,1,0:T(2,128)(2,1)} %reshape.148), calls=%async_computation | async-start | bytes 524288 | tf_op jit(solution)/shard_map/all_to_all | solution.py:47
  30.3 0.0 copy-done.3
  30.3 0.1 fusion.25
  30.3 0.1 reduce_window_sum.11
  30.4 0.2 select_reduce_fusion.1
  30.6 0.0 copy-done.5
  30.6 0.1 select_reduce_fusion
  30.7 0.7 all_to_all.46
  31.4 11.0 %all-to-all-done = bf16[32,2,2048]{2,1,0:T(2,128)(2,1)S(1)} async-done(((bf16[32,2,2048]{2,1,0:T(2,128)(2,1)}), bf16[32,2,2048]{2,1,0:T(2,128)(2,1)S(1)}, u32[]{:S(2)}, u32[]{:S(2)}) %all-to-all-start) | async-done | bytes 262176 | tf_op jit(solution)/shard_map/all_to_all | solution.py:47
  42.4 4.3 %all-to-all-start.3 = ((s32[8,1,16]{2,1,0:T(1,128)}), s32[8,1,16]{2,1,0:T(1,128)S(1)}, u32[]{:S(2)}, u32[]{:S(2)}) async-start(s32[8,1,16]{2,1,0:T(1,128)} %bitcast.9), calls=%async_computation.3 | async-start | bytes 8192 | tf_op jit(solution)/shard_map/all_to_all | solution.py:70
  46.7 0.0 copy-start.1
  46.7 0.4 reshape.149
  47.1 0.3 copy.29
  47.4 0.5 all_to_all.43
  47.9 2.3 fusion.8
  50.2 1.7 convolution_convert_fusion.1
  51.9 0.1 broadcast_in_dim.16
  52.0 0.8 reshape.107
  52.9 0.0 all-to-all-done.3
  52.9 11.6 %all_to_all.59 = bf16[8,48,256]{2,1,0:T(8,128)(2,1)S(1)} all-to-all(bf16[8,48,256]{2,1,0:T(8,128)(2,1)} %reshape.107), channel_id=1, replica_groups=mesh['tower'=8,'peer'=32] {'tower'}, dimensions={0} | all-to-all | bytes 393216 | tf_op jit(solution)/shard_map/all_to_all | solution.py:69
  64.5 0.0 copy-done.1
  64.5 4.3 %stack.2 = bf16[32,128,1024]{2,1,0:T(8,128)(2,1)} broadcast(bf16[128,1024]{1,0:T(8,128)(2,1)S(1)} %copy-done.1), dimensions={1,2} | broadcast | bytes 8650752 | tf_op jit(solution)/shard_map/stack | solution.py:11
  68.8 5.5 %all-to-all-start.2 = ((bf16[32,128,1024]{2,1,0:T(8,128)(2,1)}), bf16[32,128,1024]{2,1,0:T(8,128)(2,1)}, u32[]{:S(2)}, u32[]{:S(2)}) async-start(bf16[32,128,1024]{2,1,0:T(8,128)(2,1)} %stack.2), calls=%async_computation.2 | async-start | bytes 16777216 | tf_op jit(solution)/shard_map/all_to_all | solution.py:12
  74.3 0.2 all-gather.2.cloned.1.call-start
  74.5 0.5 all-gather.2.cloned.1.call-update
  75.0 0.6 reduce.8
  75.6 0.1 lt.53
  75.7 0.1 fusion.24
  75.8 0.2 reshape.113
  76.0 0.0 copy-done.2
  76.0 6.7 %fusion.13 = f32[384,4096]{1,0:T(8,128)} fusion(bf16[512,4096]{1,0:T(8,128)(2,1)} %param.21, bf16[384,256]{1,0:T(8,128)(2,1)S(1)} %copy-done.2, bf16[384,256]{1,0:T(8,128)(2,1)S(1)} %bitcast.40), kind=kOutput, calls=%fused_computation.30 | convolution fusion | flops 1611399168 | bytes 10878976 | tf_op jit(solution)/shard_map/dot_general | solution.py:80
  82.7 225.7 %all-to-all-done.2 = bf16[32,128,1024]{2,1,0:T(8,128)(2,1)} async-done(((bf16[32,128,1024]{2,1,0:T(8,128)(2,1)}), bf16[32,128,1024]{2,1,0:T(8,128)(2,1)}, u32[]{:S(2)}, u32[]{:S(2)}) %all-to-all-start.2) | async-done | bytes 8388640 | tf_op jit(solution)/shard_map/all_to_all | solution.py:12
  308.4 8.1 %fusion = f32[384,1024]{1,0:T(8,128)S(1)} fusion(bf16[4096,1024]{1,0:T(8,128)(2,1)} %bitcast.8, f32[384,4096]{1,0:T(8,128)} %fusion.13), kind=kOutput, calls=%fused_computation.5 | convolution fusion | flops 3229089792 | bytes 16252928 | tf_op jit(solution)/shard_map/dot_general | solution.py:82
  316.6 0.0 copy-start.6
  316.6 1.2 copy-done.6
  317.8 0.0 copy-done
  317.8 0.0 copy-done.4
  317.8 2.1 multiply_convert_fusion.3
  320.0 10.5 %fusion.5 = bf16[384,256]{1,0:T(8,128)(2,1)S(1)} fusion(bf16[512,4096]{1,0:T(8,128)(2,1)} %param.21, f32[384,4096]{1,0:T(8,128)} %fusion.13, bf16[384,1024]{1,0:T(8,128)(2,1)} %multiply_convert_fusion.3, bf16[4096,1024]{1,0:T(8,128)(2,1)} %all-gather.2.cloned.1.call-done), kind=kOutput, calls=%fused_computation.16 | convolution fusion | flops 4040785920 | bytes 17760256 | tf_op jit(solution)/shard_map/dot_general | solution.py:22
  330.5 9.2 %all_to_all.60 = bf16[8,48,256]{2,1,0:T(8,128)(2,1)S(1)} all-to-all(bf16[8,48,256]{2,1,0:T(8,128)(2,1)S(1)} %bitcast.42), channel_id=1, replica_groups=mesh['tower'=8,'peer'=32] {'tower'}, dimensions={0} | all-to-all | bytes 393216 | tf_op jit(solution)/shard_map/all_to_all | solution.py:94
  339.7 0.1 reshape.111
  339.8 0.3 reduce
  340.2 1.8 fusion.2
  341.9 3.5 fusion.1
  345.5 1.5 all_to_all.49
  346.9 0.2 copy.34
  347.2 1.1 reshape.150
  348.3 9.1 %all-to-all-start.5 = ((bf16[32,2,2048]{2,1,0:T(2,128)(2,1)}), bf16[32,2,2048]{2,1,0:T(2,128)(2,1)S(1)}, u32[]{:S(2)}, u32[]{:S(2)}) async-start(bf16[32,2,2048]{2,1,0:T(2,128)(2,1)} %reshape.150), calls=%async_computation.5 | async-start | bytes 524288 | tf_op jit(solution)/shard_map/all_to_all | solution.py:113
  357.4 3.3 multiply_convert_fusion.4
  360.7 8.5 %all-to-all-done.5 = bf16[32,2,2048]{2,1,0:T(2,128)(2,1)S(1)} async-done(((bf16[32,2,2048]{2,1,0:T(2,128)(2,1)}), bf16[32,2,2048]{2,1,0:T(2,128)(2,1)S(1)}, u32[]{:S(2)}, u32[]{:S(2)}) %all-to-all-start.5) | async-done | bytes 262176 | tf_op jit(solution)/shard_map/all_to_all | solution.py:113
  369.2 0.4 reshape.151
  369.6 5.9 %scatter_custom_fusion = bf16[2048,64]{1,0:T(8,128)(2,1)S(1)} fusion(s32[2048]{0:T(1024)S(1)} %bitcast.44, bf16[2048,64]{1,0:T(8,128)(2,1)S(1)} %bitcast.41, bf16[]{:T(256)} %constant.36.clone.1), kind=kCustom, calls=%fused_computation.35 | custom fusion | bytes 262146 | tf_op jit(solution)/shard_map/scatter | solution.py:114
  375.4 0.9 copy.32
  (7 shorter events, 0.0 us)
Async XLA Ops:
  7.2 310.6 %copy-start = (bf16[1024,1024]{1,0:T(8,128)(2,1)S(1)}, bf16[1024,1024]{1,0:T(8,128)(2,1)}, u32[]{:S(2)}) copy-start(bf16[1024,1024]{1,0:T(8,128)(2,1)} %param.23) | copy-start | bytes 6291460
  7.2 23.1 %copy-start.3 = (s32[64,1]{0,1:T(1,128)S(1)}, s32[64,1]{0,1:T(1,128)}, u32[]{:S(2)}) copy-start(s32[64,1]{0,1:T(1,128)} %param.14) | copy-start | bytes 772
  7.2 23.4 %copy-start.5 = (s32[64]{0:T(128)S(1)}, s32[64]{0:T(128)}, u32[]{:S(2)}) copy-start(s32[64]{0:T(128)} %param.15) | copy-start | bytes 772
  18.9 23.5 %all-to-all-start = ((bf16[32,2,2048]{2,1,0:T(2,128)(2,1)}), bf16[32,2,2048]{2,1,0:T(2,128)(2,1)S(1)}, u32[]{:S(2)}, u32[]{:S(2)}) async-start(bf16[32,2,2048]{2,1,0:T(2,128)(2,1)} %reshape.148), calls=%async_computation | async-start | bytes 524288 | tf_op jit(solution)/shard_map/all_to_all | solution.py:47
  42.4 10.4 %all-to-all-start.3 = ((s32[8,1,16]{2,1,0:T(1,128)}), s32[8,1,16]{2,1,0:T(1,128)S(1)}, u32[]{:S(2)}, u32[]{:S(2)}) async-start(s32[8,1,16]{2,1,0:T(1,128)} %bitcast.9), calls=%async_computation.3 | async-start | bytes 8192 | tf_op jit(solution)/shard_map/all_to_all | solution.py:70
  46.7 17.8 %copy-start.1 = (bf16[128,1024]{1,0:T(8,128)(2,1)S(1)}, bf16[128,1024]{1,0:T(8,128)(2,1)}, u32[]{:S(2)}) copy-start(bf16[128,1024]{1,0:T(8,128)(2,1)} %param.22) | copy-start | bytes 786436
  68.8 7.2 %copy-start.2 = (bf16[384,256]{1,0:T(8,128)(2,1)S(1)}, bf16[384,256]{1,0:T(8,128)(2,1)}, u32[]{:S(2)}) copy-start(bf16[384,256]{1,0:T(8,128)(2,1)} %param.16) | copy-start | bytes 589828
  68.8 239.7 %all-to-all-start.2 = ((bf16[32,128,1024]{2,1,0:T(8,128)(2,1)}), bf16[32,128,1024]{2,1,0:T(8,128)(2,1)}, u32[]{:S(2)}, u32[]{:S(2)}) async-start(bf16[32,128,1024]{2,1,0:T(8,128)(2,1)} %stack.2), calls=%async_computation.2 | async-start | bytes 16777216 | tf_op jit(solution)/shard_map/all_to_all | solution.py:12
  74.3 245.7 %all-gather.2.cloned.1.call-start = ((), (), s32[]{:S(2)}) async-start(), calls=%async_computation.6 | async-start | bytes 8650752 | tf_op jit(solution)/shard_map/all_gather | solution.py:91
  308.4 9.4 %copy-start.4 = (bf16[384,1024]{1,0:T(8,128)(2,1)S(1)}, bf16[384,1024]{1,0:T(8,128)(2,1)}, u32[]{:S(2)}) copy-start(bf16[384,1024]{1,0:T(8,128)(2,1)} %param.17) | copy-start | bytes 2359300
  316.6 1.2 copy-start.6
  348.3 20.9 %all-to-all-start.5 = ((bf16[32,2,2048]{2,1,0:T(2,128)(2,1)}), bf16[32,2,2048]{2,1,0:T(2,128)(2,1)S(1)}, u32[]{:S(2)}, u32[]{:S(2)}) async-start(bf16[32,2,2048]{2,1,0:T(2,128)(2,1)} %reshape.150), calls=%async_computation.5 | async-start | bytes 524288 | tf_op jit(solution)/shard_map/all_to_all | solution.py:113
Sparse Core Ops, SparseCore 0:
  77.7 222.9 all-gather.1
